TPU v7x, 32 devices: a whole 2x2x4 slice. The times are simulated.
32 devices in a mesh: seq: 16 (over z, y, x), head: 2 (over core).
Axes of the slice: x: 2, y: 2, z: 4, core: 2. Of those that a mesh axis runs over, the one named last changes fastest.
Arguments:
- queries: bfloat16 [8192, 4096], P('seq', 'head'), may hold values from -10 to 10
- keys: bfloat16 [8192, 4096], P('seq', 'head'), may hold values from -4.5 to 7
- values: bfloat16 [8192, 4096], P('seq', 'head'), may hold values from -8 to 8
- gate_bias: float32 [32], P('head'), may hold values from -3 to 3
- out_weight: bfloat16 [4096, 4096], P('head'), may hold values from -0.09375 to 0.09375
Outputs:
- mixed: bfloat16 [8192, 4096], P(('seq', 'head'))
All inputs are finite; a program needn't handle non-finite values.
Results may differ from a plain program's by a relative error of at most 0.004.
The roundings to bfloat16 on the way count: a program that leaves them out, or rounds other values in their place, can miss the bound.
Values sent between devices are 32-bit elements; how exact they have to be, the bound alone decides.
A program may use at most 256 MiB of HBM per device.

v0:
```python
import jax
import jax.numpy as jnp
from jax import lax
from jax.sharding import PartitionSpec as P

SEG = 512


def carried_in(x, axis, combine, identity):
    count, place = (lax.axis_size(axis), lax.axis_index(axis))
    everything = jax.tree.map(lambda part: lax.all_gather(part, axis), x)
    start = jax.tree.map(
        lambda part, zero: jnp.broadcast_to(jnp.asarray(zero, part.dtype), part.shape), x, identity
    )

    def turn(k, before):
        reached = k < place
        new = combine(before, jax.tree.map(lambda part: part[k], everything))
        return jax.tree.map(lambda a, b: jnp.where(reached, a, b), new, before)

    return lax.fori_loop(0, count, turn, start)


def lifted(source):
    return jnp.where(source > 0, source + 1.0, jnp.exp(jnp.minimum(source, 0.0)))


def add_pair(earlier, later):
    return (earlier[0] + later[0], earlier[1] + later[1])


def on_device(queries, keys, values, gate_bias, out_weight):
    head_count = gate_bias.shape[0]
    feat_width = queries.shape[1]
    head_size = feat_width // head_count
    seg_count = queries.shape[0] // SEG
    query_blocks = queries.reshape(seg_count, SEG, head_count, head_size)
    key_blocks = keys.reshape(seg_count, SEG, head_count, head_size)
    value_blocks = values.reshape(seg_count, SEG, head_count, head_size)
    lift_query = lifted(query_blocks.astype(jnp.float32)).astype(jnp.bfloat16)
    lift_key = lifted(key_blocks.astype(jnp.float32)).astype(jnp.bfloat16)
    updates = jnp.einsum(
        "sqhd,sqhe->shde", lift_key, value_blocks, preferred_element_type=jnp.float32
    )
    norm_adds = jnp.sum(lift_key.astype(jnp.float32), axis=1)
    own_memory = jnp.sum(updates, axis=0)
    own_norm = jnp.sum(norm_adds, axis=0)
    zero_state = (jnp.zeros_like(own_memory), jnp.zeros_like(own_norm))
    memory, normalizer = carried_in((own_memory, own_norm), "seq", add_pair, zero_state)
    scores = jnp.einsum(
        "sqhd,skhd->shqk", query_blocks, key_blocks, preferred_element_type=jnp.float32
    ) / jnp.sqrt(jnp.float32(head_size))
    causal = jnp.arange(SEG)[:, None] >= jnp.arange(SEG)[None, :]
    scores = jnp.where(causal[None, None], scores, -jnp.inf)
    top_score = jnp.max(scores, axis=-1, keepdims=True)
    expo = jnp.exp(scores - top_score)
    weights = (expo / jnp.sum(expo, axis=-1, keepdims=True)).astype(jnp.bfloat16)
    local_part = jnp.einsum(
        "shqk,skhd->sqhd", weights, value_blocks, preferred_element_type=jnp.float32
    )
    mix_gate = jax.nn.sigmoid(gate_bias)[None, :, None]
    numerator = jnp.einsum(
        "qhd,hde->qhe",
        lift_query[0],
        memory.astype(jnp.bfloat16),
        preferred_element_type=jnp.float32,
    )
    denominator = jnp.einsum(
        "qhd,hd->qh", lift_query[0].astype(jnp.float32), normalizer, precision=lax.Precision.HIGHEST
    )
    mem_read = numerator / jnp.maximum(denominator, 1.0)[..., None]
    segment_outs = [(mix_gate * mem_read + (1.0 - mix_gate) * local_part[0]).astype(jnp.bfloat16)]
    attn = jnp.stack(segment_outs).reshape(seg_count * SEG, feat_width)
    mixed = lax.psum_scatter(
        jnp.dot(attn, out_weight, preferred_element_type=jnp.float32),
        "head",
        scatter_dimension=0,
        tiled=True,
    )
    return mixed.astype(jnp.bfloat16)


def solution(mesh):
    in_specs = (P("seq", "head"), P("seq", "head"), P("seq", "head"), P("head"), P("head", None))
    out_specs = P(("seq", "head"), None)
    return jax.shard_map(
        on_device, mesh=mesh, in_specs=in_specs, out_specs=out_specs, check_vma=False
    )
```

profile of v0, /device:TPU:25, one launch (start us, length us, event | category | flops | bytes accessed | tf_op | source)
XLA Modules:
  0.0 288.1 jit_solution(3639902188622813780)
XLA Ops:
  6.5 4.1 %copy.29 = bf16[512,2048]{0,1:T(8,128)(2,1)} copy(bf16[512,2048]{1,0:T(8,128)(2,1)} %param.9) | data formatting | bytes 4194304 | tf_op jit(solution)/shard_map/reshape.1
  10.6 4.5 %fusion.18 = f32[16,128,128]{2,1,0:T(8,128)} fusion(bf16[512,16,128]{0,2,1:T(8,128)(2,1)} %bitcast.74, bf16[512,2048]{1,0:T(8,128)(2,1)} %param.8), kind=kOutput, calls=%fused_computation.35 | convolution fusion | flops 274726912 | bytes 5242880 | tf_op jit(solution)/shard_map/sqhd,sqhe->shde/dot_general | solution.py:42
  15.2 0.0 reduce-scatter.2.cloned.1.call-start
  15.3 2.7 convert_reduce_fusion
  17.9 29.4 %all_gather.9 = f32[16,16,128]{2,1,0:T(8,128)S(1)} all-gather(f32[1,16,128]{2,1,0:T(8,128)S(1)} %bitcast.78), channel_id=1, replica_groups=mesh['seq'=16,'head'=2] {'seq'}, dimensions={0}, use_global_device_ids=true | all-gather | bytes 139264 | tf_op jit(solution)/shard_map/all_gather | solution.py:11
  47.3 0.1 iota_compare_fusion
  47.5 9.6 %fusion.20 = f32[16,512,512]{1,2,0:T(8,128)} fusion(bf16[512,2048]{1,0:T(8,128)(2,1)S(1)} %copy-done, bf16[512,2048]{1,0:T(8,128)(2,1)} %param.8), kind=kOutput, calls=%fused_computation.36 | convolution fusion | flops 1073741824 | bytes 20971520 | tf_op jit(solution)/shard_map/sqhd,skhd->shqk/dot_general | solution.py:50
  57.1 19.5 %fusion.43 = (f32[16,512]{1,0:T(8,128)S(1)}, f32[16,512,512]{1,2,0:T(8,128)}) fusion(f32[16,512,512]{1,2,0:T(8,128)} %fusion.20, pred[512,512]{0,1:T(8,128)(4,1)S(1)} %iota_compare_fusion), kind=kOutput, calls=%fused_computation.61 | output fusion | flops 25166336 | bytes 33849344 | tf_op jit(solution)/shard_map/sub | solution.py:56
  76.6 130.7 %all-gather.3.cloned.1.call-done = f32[256,128,128]{2,1,0:T(8,128)} async-done(((f32[16,128,128]{2,1,0:T(8,128)}), f32[256,128,128]{2,1,0:T(8,128)}) %all-gather.3.cloned.1.call-update) | async-done | bytes 16777232 | tf_op jit(solution)/shard_map/all_gather | solution.py:11
  207.3 26.1 %while.16 = (s32[]{:T(128)}, f32[16,128,128]{2,1,0:T(8,128)S(1)}, f32[16,128]{1,0:T(8,128)S(1)}, s32[]{:T(128)}, f32[16,16,128,128]{3,2,1,0:T(8,128)}, /*index=5*/f32[16,16,128]{2,1,0:T(8,128)S(1)}, s32[]{:T(128)}, s32[]{:T(128)}) while((s32[]{:T(128)}, f32[16,128,128]{2,1,0:T(8,128)S(1)}, f32[16,128]{1,0:T(8,128)S(1)}, s32[]{:T(128)}, ...), condition=%wide.region_2.3_spmd.clone, body=%wide.region_1.2_spmd.clone.sunk | while | flops 792580 | bytes 3170427 | solution.py:21
  207.3 1.6 add_select_fusion.4
  208.9 1.6 add_select_fusion.4
  210.6 1.6 add_select_fusion.4
  212.2 1.6 add_select_fusion.4
  213.8 1.6 add_select_fusion.4
  215.5 1.6 add_select_fusion.4
  217.1 1.6 add_select_fusion.4
  218.8 1.6 add_select_fusion.4
  220.4 1.6 add_select_fusion.4
  222.0 1.6 add_select_fusion.4
  223.7 1.6 add_select_fusion.4
  225.3 1.6 add_select_fusion.4
  226.9 1.6 add_select_fusion.4
  228.6 1.6 add_select_fusion.4
  230.2 1.6 add_select_fusion.4
  231.8 1.6 add_select_fusion.4
  233.5 1.3 fusion.31
  234.8 2.2 fusion.29
  237.0 8.0 %fusion.16 = bf16[512,16,128]{0,2,1:T(8,128)(2,1)S(1)} fusion(f32[16,128,512]{2,1,0:T(8,128)S(1)} %fusion.31, bf16[512,16,128]{0,2,1:T(8,128)(2,1)S(1)} %bitcast.75, f32[16,512,512]{1,2,0:T(8,128)} %get-tuple-element.153, f32[16,512]{1,0:T(8,128)S(1)} %get-tuple-element.152, f32[16]{0:T(128)S(1)} %get-tuple-element.150, f32[512,16]{0,1:T(8,128)S(1)} %fusion.34, ...), kind=kOutput, calls=%fused_computation.31 | convolution fusion | flops 1087373312 | bytes 25231488 | tf_op jit(solution)/shard_map/shqk,skhd->sqhd/dot_general | solution.py:58
  245.0 14.9 %fusion.44 = f32[512,4096]{1,0:T(8,128)} fusion(bf16[512,2048]{0,1:T(8,128)(2,1)S(1)} %bitcast.79, bf16[2048,4096]{1,0:T(8,128)(2,1)} %param.11), kind=kOutput, calls=%fused_computation.62 | convolution fusion | flops 8589934592 | bytes 27262976 | tf_op jit(solution)/shard_map/dot_general | solution.py:75
  259.9 17.6 %reduce-scatter.2.cloned.1.call-done = f32[256,4096]{1,0:T(8,128)} async-done(((f32[512,4096]{1,0:T(8,128)}), f32[256,4096]{1,0:T(8,128)}) %reduce-scatter.2.cloned.1.call-update) | async-done | bytes 4194320 | tf_op jit(solution)/shard_map/reduce_scatter | solution.py:74
  277.5 3.8 %convert_element_type.62 = bf16[256,4096]{1,0:T(8,128)(2,1)} convert(f32[256,4096]{1,0:T(8,128)} %reduce-scatter.2.cloned.1.call-done) | non-fusion elementwise | flops 1048576 | bytes 6291456 | tf_op jit(solution)/shard_map/convert_element_type | solution.py:80
  (31 shorter events, 0.3 us)
Async XLA Ops:
  6.5 40.9 %copy-start = (bf16[512,2048]{1,0:T(8,128)(2,1)S(1)}, bf16[512,2048]{1,0:T(8,128)(2,1)}, u32[]{:S(2)}) copy-start(bf16[512,2048]{1,0:T(8,128)(2,1)} %param.7) | copy-start | bytes 6291460
  6.5 200.8 %all-gather.3.cloned.1.call-start = ((), (), s32[]{:S(2)}) async-start(), calls=%async_computation.2 | async-start | bytes 17825792 | tf_op jit(solution)/shard_map/all_gather | solution.py:11
  10.6 36.8 %copy-start.3 = (f32[16]{0:T(128)S(1)}, f32[16]{0:T(128)}, u32[]{:S(2)}) copy-start(f32[16]{0:T(128)} %param.10) | copy-start | bytes 196
  15.2 262.3 %reduce-scatter.2.cloned.1.call-start = ((), (), s32[]{:S(2)}) async-start(), calls=%async_computation.1 | async-start | bytes 12582912 | tf_op jit(solution)/shard_map/reduce_scatter | solution.py:74
  234.8 2.3 copy-start.2
  259.9 21.4 %copy-start.1 = (bf16[512,2048]{1,0:T(8,128)(2,1)S(1)}, bf16[512,2048]{1,0:T(8,128)(2,1)}, u32[]{:S(2)}) copy-start(bf16[512,2048]{1,0:T(8,128)(2,1)} %param.7) | copy-start | bytes 6291460
Sparse Core Ops, SparseCore 0:
  15.3 191.9 all-gather.2
  260.0 17.4 reduce-scatter.1
where the time goes:
time: 290 us; the launch traced here: 288 us
  waiting for transfers between devices  148 us (51%)
  other arithmetic  51.7 us (18%)
  matrix products  40.5 us (14%)
  blocking collectives  29.4 us (10%)
  between operations  13.5 us (5%)
  local copies, waits for them, and re-layouts  4.08 us (1%)
    all_gather x1, waiting for transfers between devices, carried_in(): everything = jax.tree.map(lambda part: lax.all_gather(part, axis), x)  131 us
    all_gather x1, blocking collectives, carried_in(): everything = jax.tree.map(lambda part: lax.all_gather(part, axis), x)  29.4 us
    select_n x32, other arithmetic, turn(): return jax.tree.map(lambda a, b: jnp.where(reached, a, b), new, before)  25.6 us
    sub x1, other arithmetic, on_device(): expo = jnp.exp(scores - top_score)  19.5 us
    reduce_scatter x1, waiting for transfers between devices, on_device(): lax.psum_scatter(jnp.dot(attn, out_weight, preferred_element_type=jnp.flo...  17.6 us
    dot_general x1, matrix products, on_device(): jnp.dot(attn, out_weight, preferred_element_type=jnp.float32)  14.9 us
    dot_general x1, matrix products, on_device(): jnp.einsum('sqhd,skhd->shqk', query_blocks, key_blocks, preferred_element...  9.65 us
    dot_general x1, matrix products, on_device(): jnp.einsum('shqk,skhd->sqhd', weights, value_blocks, preferred_element_ty...  7.96 us
  transfers between devices with their start and end apart: 2, of which 2 were waited for; matrix products, arithmetic and copies ran while one was open for 11% of the time, Pallas kernels for 0%

commit v1 on v0

v1 whole, which is shorter than its diff:
```python
import functools

import jax
import jax.numpy as jnp
from jax import lax
from jax.experimental import pallas as pl
from jax.experimental.pallas import tpu as pltpu
from jax.sharding import PartitionSpec as P

SEG = 512
MESH = pl.DeviceIdType.MESH
F32 = jnp.float32
BF16 = jnp.bfloat16


def lifted(source):
    return jnp.where(source > 0, source + 1.0, jnp.exp(jnp.minimum(source, 0.0)))


def dot(a, b, dims):
    return lax.dot_general(a, b, ((dims[:1], dims[1:]), ((), ())), preferred_element_type=F32)


class Line:
    def __init__(self, size, place, device, refs):
        self.size, self.place, self.device = size, place, device
        if size == 2:
            self.inbox, self.send, self.recv = refs
        else:
            (self.right_in, self.left_in, self.right_out, self.left_out,
             self.right_send, self.right_recv, self.left_send, self.left_recv) = refs

    def swap(self, src, h):
        return pltpu.make_async_remote_copy(
            src.at[h], self.inbox.at[h], self.send.at[h], self.recv.at[h],
            device_id=self.device(1 - self.place), device_id_type=MESH)

    def to_right(self, src, h):
        return pltpu.make_async_remote_copy(
            src.at[h], self.right_in.at[h], self.right_send.at[h], self.right_recv.at[h],
            device_id=self.device(jnp.minimum(self.place + 1, self.size - 1)), device_id_type=MESH)

    def to_left(self, src, h):
        return pltpu.make_async_remote_copy(
            src.at[h], self.left_in.at[h], self.left_send.at[h], self.left_recv.at[h],
            device_id=self.device(jnp.maximum(self.place - 1, 0)), device_id_type=MESH)

    def begin(self, src, h):
        if self.size == 2:
            self.swap(src, h).start()
            return

        @pl.when(self.place == 0)
        def _():
            self.to_right(src, h).start()

        @pl.when(self.place == self.size - 1)
        def _():
            self.to_left(src, h).start()

    def finish(self, src, before, total, h, add):
        if self.size == 2:
            self.swap(src, h).wait_recv()
            got = self.inbox[h]
            total[h] = src[h] + got
            earlier = jnp.where(self.place > 0, got, jnp.zeros_like(got))
            before[h] = before[h] + earlier if add else earlier
            return
        place, last = self.place, self.size - 1
        total[h] = src[h]
        if not add:
            before[h] = jnp.zeros(before.shape[1:], F32)

        @pl.when(place > 0)
        def _():
            self.to_right(src, h).wait_recv()
            got = self.right_in[h]
            before[h] = before[h] + got
            total[h] = total[h] + got

            @pl.when(place < last)
            def _():
                self.right_out[h] = got + src[h]
                self.to_right(self.right_out, h).start()

        @pl.when(place < last)
        def _():
            self.to_left(src, h).wait_recv()
            got = self.left_in[h]
            total[h] = total[h] + got

            @pl.when(place > 0)
            def _():
                self.left_out[h] = got + src[h]
                self.to_left(self.left_out, h).start()

    def drain(self, src, h):
        if self.size == 2:
            self.swap(src, h).wait_send()
            return

        @pl.when(self.place < self.size - 1)
        def _():
            self.to_right(src, h).wait_send()

        @pl.when(self.place > 0)
        def _():
            self.to_left(src, h).wait_send()


def line_scratch(size, heads, state):
    box = pltpu.VMEM((heads,) + state, F32)
    sem = pltpu.SemaphoreType.DMA((heads,))
    return [box, sem, sem] if size == 2 else [box] * 4 + [sem] * 4


GROUP = 4


def kernel(sizes, tile, gate, q_hbm, k_hbm, v_hbm, w_hbm, o_hbm, *scratch):
    x_size, y_size, z_size = sizes
    scratch = list(scratch)

    def take(count):
        taken = scratch[:count]
        del scratch[:count]
        return taken

    qb, kb, vb, wb, loc, attn, acc, peer, outb = take(9)
    own, row_sum, plane_sum, before, z_in = take(5)
    q_sem, k_sem, v_sem, w_sem, o_sem = take(5)
    z_send, z_recv, peer_send, peer_recv = take(4)
    x_refs = take(3 if x_size == 2 else 8)
    y_refs = take(3 if y_size == 2 else 8)

    heads, rows, width = qb.shape
    half = rows // 2
    tiles = acc.shape[0]
    depth = GROUP * width
    groups = heads // GROUP
    seq, core = lax.axis_index("seq"), lax.axis_index("head")
    x = lax.rem(seq, x_size)
    y = lax.rem(seq // x_size, y_size)
    z = seq // (x_size * y_size)

    def at(xx, yy, zz):
        return ((zz * y_size + yy) * x_size + xx, core)

    x_line = Line(x_size, x, lambda c: at(c, y, z), x_refs)
    y_line = Line(y_size, y, lambda c: at(x, c, z), y_refs)
    other = 1 - core

    def load(src, dst, sem, h):
        return pltpu.make_async_copy(
            src.at[:, pl.ds(pl.multiple_of(h * width, width), width)], dst.at[h], sem.at[h])

    def load_w(g):
        part = pl.ds(pl.multiple_of(g * depth, depth), depth)
        return pltpu.make_async_copy(w_hbm.at[part, :], wb.at[part, :], w_sem.at[g])

    def start_loads(h, _):
        load(k_hbm, kb, k_sem, h).start()
        load(v_hbm, vb, v_sem, h).start()
        return 0

    def start_queries(h, _):
        load(q_hbm, qb, q_sem, h).start()
        return 0

    def start_weights(g, _):
        load_w(g).start()
        return 0

    lax.fori_loop(0, heads, start_loads, 0)
    lax.fori_loop(0, heads, start_queries, 0)
    lax.fori_loop(0, groups, start_weights, 0)

    barrier = pltpu.get_barrier_semaphore()
    pl.semaphore_signal(barrier, inc=1, device_id=(seq, other), device_id_type=MESH)
    greeted = 1
    for place, size, where in (
        (x, x_size, lambda c: at(c, y, z)),
        (y, y_size, lambda c: at(x, c, z)),
        (z, z_size, lambda c: at(x, y, c)),
    ):
        @pl.when(place > 0)
        def _():
            pl.semaphore_signal(barrier, inc=1, device_id=where(place - 1), device_id_type=MESH)

        @pl.when(place < size - 1)
        def _():
            pl.semaphore_signal(barrier, inc=1, device_id=where(place + 1), device_id_type=MESH)

        greeted = greeted + (place > 0).astype(jnp.int32) + (place < size - 1).astype(jnp.int32)
    pl.semaphore_wait(barrier, greeted)

    def z_copy(src, h):
        return pltpu.make_async_remote_copy(
            src.at[h], z_in.at[h], z_send.at[h], z_recv.at[h],
            device_id=at(x, y, jnp.minimum(z + 1, z_size - 1)), device_id_type=MESH)

    def update(h):
        load(k_hbm, kb, k_sem, h).wait()
        load(v_hbm, vb, v_sem, h).wait()
        lift_key = lifted(kb[h].astype(F32)).astype(BF16)
        own[h, pl.ds(0, width), :] = dot(lift_key, vb[h], (0, 0))
        zsum = jnp.sum(lift_key.astype(F32), axis=0, keepdims=True)
        own[h, pl.ds(width, 8), :] = jnp.broadcast_to(zsum, (8, width))
        x_line.begin(own, h)

    def local(h):
        load(q_hbm, qb, q_sem, h).wait()
        rate = 1.4426950408889634 / (width ** 0.5)
        keep = 1.0 / (1.0 + jnp.exp(jnp.full((1, width), gate[h], F32)))
        causal = (lax.broadcasted_iota(jnp.int32, (half, half), 0)
                  >= lax.broadcasted_iota(jnp.int32, (half, half), 1))
        for part in range(2):
            rows_here = pl.ds(part * half, half)
            qs = qb[h, rows_here, :]
            diag = jnp.where(causal, dot(qs, kb[h, rows_here, :], (1, 1)), -jnp.inf)
            top = jnp.max(diag, axis=-1, keepdims=True)
            if part == 1:
                past = dot(qs, kb[h, pl.ds(0, half), :], (1, 1))
                top = jnp.maximum(top, jnp.max(past, axis=-1, keepdims=True))
                past = jnp.exp2((past - top) * rate)
            diag = jnp.exp2((diag - top) * rate)
            total = jnp.sum(diag, axis=-1, keepdims=True)
            if part == 1:
                total = total + jnp.sum(past, axis=-1, keepdims=True)
            inverse = 1.0 / total
            out = dot((diag * inverse).astype(BF16), vb[h, rows_here, :], (1, 0))
            if part == 1:
                out = out + dot((past * inverse).astype(BF16), vb[h, pl.ds(0, half), :], (1, 0))
            loc[h, rows_here, :] = out * keep

    def z_stage(h):
        @pl.when(z > 0)
        def _():
            z_copy(plane_sum, h).wait_recv()
            got = z_in[h]
            before[h] = before[h] + got
            plane_sum[h] = plane_sum[h] + got

        @pl.when(z < z_size - 1)
        def _():
            z_copy(plane_sum, h).start()

    def read(h):
        share = 1.0 / (1.0 + jnp.exp(jnp.full((1, width), -gate[h], F32)))
        lift_query = lifted(qb[h].astype(F32)).astype(BF16)
        memory = before[h, pl.ds(0, width), :].astype(BF16)
        numerator = dot(lift_query, memory, (1, 0))
        norm = before[h, pl.ds(width, 1), :]
        denominator = jnp.sum(lift_query.astype(F32) * norm, axis=-1, keepdims=True)
        inverse = 1.0 / jnp.maximum(denominator, 1.0)
        value = numerator * inverse * share + loc[h]
        attn[:, pl.ds(pl.multiple_of(h * width, width), width)] = value.astype(BF16)

    def columns(n):
        return pl.ds(pl.multiple_of(n * tile, tile), tile)

    def project(g):
        load_w(g).wait()
        part = pl.ds(pl.multiple_of(g * depth, depth), depth)

        def one(n, _):
            product = dot(attn[:, part], wb[part, columns(n)], (1, 0))

            @pl.when(g == 0)
            def _():
                acc[n] = product

            @pl.when(g > 0)
            def _():
                acc[n] = acc[n] + product
            return 0

        lax.fori_loop(0, tiles, one, 0)

    x_lag, y_lag = 1, 2
    z_lag = y_lag + 2 * z

    def within(h):
        return jnp.logical_and(h >= 0, h < heads)

    def step(i, _):
        @pl.when(2 * i < heads)
        def _():
            update(2 * i)
            update(2 * i + 1)

        @pl.when(within(i - x_lag))
        def _():
            h = i - x_lag
            x_line.finish(own, before, row_sum, h, False)
            y_line.begin(row_sum, h)

        @pl.when(within(i - y_lag))
        def _():
            y_line.finish(row_sum, before, plane_sum, i - y_lag, True)

        @pl.when(within(i - z_lag))
        def _():
            z_stage(i - z_lag)

        @pl.when(i < heads)
        def _():
            local(i)

        @pl.when(within(i - z_lag))
        def _():
            h = i - z_lag
            read(h)

            @pl.when(jnp.logical_and(lax.rem(h, GROUP) == GROUP - 1, h < heads - 1))
            def _():
                project(h // GROUP)
        return 0

    lax.fori_loop(0, heads + y_lag + 2 * (z_size - 1), step, 0)

    last = pl.ds((groups - 1) * depth, depth)
    load_w(groups - 1).wait()
    theirs = pl.ds(pl.multiple_of(other * half, half), half)
    mine = pl.ds(pl.multiple_of(core * half, half), half)

    def to_peer(n):
        return pltpu.make_async_remote_copy(
            acc.at[n, theirs, :], peer.at[n], peer_send.at[n], peer_recv.at[n],
            device_id=(seq, other), device_id_type=MESH)

    def result(n):
        return pltpu.make_async_copy(outb.at[:, columns(n)], o_hbm.at[:, columns(n)], o_sem.at[n])

    def send_tile(n, _):
        acc[n, theirs, :] = acc[n, theirs, :] + dot(attn[theirs, last], wb[last, columns(n)], (1, 0))
        to_peer(n).start()
        return 0

    def own_tile(n, _):
        value = acc[n, mine, :] + dot(attn[mine, last], wb[last, columns(n)], (1, 0))
        to_peer(n).wait_recv()
        outb[:, columns(n)] = (value + peer[n]).astype(BF16)
        result(n).start()
        return 0

    lax.fori_loop(0, tiles, send_tile, 0)
    lax.fori_loop(0, tiles, own_tile, 0)

    def drain(h, _):
        x_line.drain(own, h)
        y_line.drain(row_sum, h)

        @pl.when(z < z_size - 1)
        def _():
            z_copy(plane_sum, h).wait_send()
        return 0

    def drain_tiles(n, _):
        to_peer(n).wait_send()
        result(n).wait()
        return 0

    lax.fori_loop(0, heads, drain, 0)
    lax.fori_loop(0, tiles, drain_tiles, 0)


def on_device(sizes, queries, keys, values, gate_bias, out_weight):
    heads = gate_bias.shape[0]
    rows, feat = queries.shape
    width = feat // heads
    model = out_weight.shape[1]
    tile = 512
    tiles = model // tile
    state = (width + 8, width)
    box = pltpu.VMEM((heads,) + state, F32)
    sem = pltpu.SemaphoreType.DMA((heads,))
    tile_sem = pltpu.SemaphoreType.DMA((tiles,))
    blocks = pltpu.VMEM((heads, rows, width), BF16)
    scratch = [
        blocks, blocks, blocks,
        pltpu.VMEM(out_weight.shape, BF16),
        pltpu.VMEM((heads, rows, width), F32),
        pltpu.VMEM((rows, feat), BF16),
        pltpu.VMEM((tiles, rows, tile), F32),
        pltpu.VMEM((tiles, rows // 2, tile), F32),
        pltpu.VMEM((rows // 2, model), BF16),
        box, box, box, box, box,
        sem, sem, sem, pltpu.SemaphoreType.DMA((heads // GROUP,)), tile_sem,
        sem, sem, tile_sem, tile_sem,
    ] + line_scratch(sizes[0], heads, state) + line_scratch(sizes[1], heads, state)
    hbm = pl.BlockSpec(memory_space=pl.ANY)
    return pl.pallas_call(
        functools.partial(kernel, sizes, tile),
        out_shape=jax.ShapeDtypeStruct((rows // 2, model), BF16),
        in_specs=[pl.BlockSpec(memory_space=pltpu.SMEM), hbm, hbm, hbm, hbm],
        out_specs=hbm,
        scratch_shapes=scratch,
        compiler_params=pltpu.CompilerParams(
            collective_id=0, has_side_effects=True, vmem_limit_bytes=62 * 1024 * 1024),
        cost_estimate=pl.CostEstimate(
            flops=2 * rows * feat * (model + rows + 2 * width), bytes_accessed=24 * 1024 * 1024,
            transcendentals=heads * rows * rows),
    )(gate_bias, queries, keys, values, out_weight)


def grid_of(count):
    z_size = min(4, count)
    plane = count // z_size
    y_size = 1
    while y_size * y_size < plane:
        y_size *= 2
    return (plane // y_size, y_size, z_size)


def solution(mesh):
    in_specs = (P("seq", "head"), P("seq", "head"), P("seq", "head"), P("head"), P("head", None))
    out_specs = P(("seq", "head"), None)
    return jax.shard_map(
        functools.partial(on_device, grid_of(mesh.shape["seq"])),
        mesh=mesh, in_specs=in_specs, out_specs=out_specs, check_vma=False
    )
```

time: 290 us -> 81.1 us (0.28)
  waiting for transfers between devices: 148 us -> 0 us
  Pallas kernels: 0 us -> 77.8 us
  other arithmetic: 51.7 us -> 0 us
  matrix products: 40.5 us -> 0 us
  blocking collectives: 29.4 us -> 0 us
  between operations: 13.5 us -> 0.01 us
    all_gather x1 -> x0, waiting for transfers between devices: 131 us -> none  [carried_in(): everything = jax.tree.map(lambda part: lax.all_gather(part, axis), x)]
    pallas_call x0 -> x1, Pallas kernels: none -> 77.8 us  [on_device(): pl.pallas_call(functools.partial(kernel, sizes, tile), out_shape=jax.Shap...]
    dot_general x6 -> x0, matrix products: 40.5 us -> none  [the longest x1 14.9 us: on_device(): jnp.dot(attn, out_weight, preferred_element_type=jnp.float32)]
    all_gather x1 -> x0, blocking collectives: 29.4 us -> none  [carried_in(): everything = jax.tree.map(lambda part: lax.all_gather(part, axis), x)]
    select_n x32 -> x0, other arithmetic: 25.6 us -> none  [turn(): return jax.tree.map(lambda a, b: jnp.where(reached, a, b), new, before)]
    sub x2 -> x0, other arithmetic: 19.5 us -> none  [the longest x1 19.5 us: on_device(): expo = jnp.exp(scores - top_score)]
    reduce_scatter x1 -> x0, waiting for transfers between devices: 17.6 us -> none  [on_device(): lax.psum_scatter(jnp.dot(attn, out_weight, preferred_element_type=jnp.flo...]
    another operation x1 -> x0, local copies, waits for them, and re-layouts: 4.06 us -> none
  transfers between devices with their start and end apart: 2 -> 0, of which waited for: 2 -> 0; matrix products, arithmetic and copies ran while one was open for 11% -> 0% of each run, Pallas kernels for 0% -> 0%
where the time goes in v1:
time: 81.1 us; the launch traced here: 80.9 us
  Pallas kernels  77.8 us (96%)
  local copies, waits for them, and re-layouts  3.13 us (4%)
    pallas_call x1, Pallas kernels, on_device(): pl.pallas_call(functools.partial(kernel, sizes, tile), out_shape=jax.Shap...  77.8 us
    unnamed x1, local copies, waits for them, and re-layouts  3.13 us

profile of v1, /device:TPU:25, one launch (start us, length us, event | category | flops | bytes accessed | tf_op | source)
XLA Modules:
  0.0 80.9 jit_solution(7864919769778315330)
XLA Ops:
  0.0 77.8 %shard_map.55 = bf16[256,4096]{1,0:T(8,128)(2,1)} custom-call(f32[16]{0:T(128)} %gate.1, bf16[512,2048]{1,0:T(8,128)(2,1)} %q_hbm.1, bf16[512,2048]{1,0:T(8,128)(2,1)} %k_hbm.1, bf16[512,2048]{1,0:T(8,128)(2,1)} %v_hbm.1, bf16[2048,4096]{1,0:T(8,128)(2,1)} %w_hbm.1), custom_call_target="tpu_custom_call" | custom-call | flops 10200547328 | bytes 25165824 | tf_op jit(solution)/shard_map/pallas_call | solution.py:393
  77.8 3.1 %copy.7 = bf16[256,4096]{1,0:T(8,128)(2,1)} copy(bf16[256,4096]{1,0:T(8,128)(2,1)} %shard_map.55) | data formatting | bytes 4194304

commit v2 on v1

--- a/solution.py
+++ b/solution.py
@@ -114,7 +114,7 @@
     return [box, sem, sem] if size == 2 else [box] * 4 + [sem] * 4
 
 
-GROUP = 4
+GROUP = 8
 
 
 def kernel(sizes, tile, gate, q_hbm, k_hbm, v_hbm, w_hbm, o_hbm, *scratch):
@@ -200,16 +200,12 @@
             device_id=at(x, y, jnp.minimum(z + 1, z_size - 1)), device_id_type=MESH)
 
     def update(h):
-        load(k_hbm, kb, k_sem, h).wait()
-        load(v_hbm, vb, v_sem, h).wait()
         lift_key = lifted(kb[h].astype(F32)).astype(BF16)
         own[h, pl.ds(0, width), :] = dot(lift_key, vb[h], (0, 0))
         zsum = jnp.sum(lift_key.astype(F32), axis=0, keepdims=True)
         own[h, pl.ds(width, 8), :] = jnp.broadcast_to(zsum, (8, width))
-        x_line.begin(own, h)
 
     def local(h):
-        load(q_hbm, qb, q_sem, h).wait()
         rate = 1.4426950408889634 / (width ** 0.5)
         keep = 1.0 / (1.0 + jnp.exp(jnp.full((1, width), gate[h], F32)))
         causal = (lax.broadcasted_iota(jnp.int32, (half, half), 0)
@@ -239,11 +235,11 @@
             z_copy(plane_sum, h).wait_recv()
             got = z_in[h]
             before[h] = before[h] + got
-            plane_sum[h] = plane_sum[h] + got
-
-        @pl.when(z < z_size - 1)
-        def _():
-            z_copy(plane_sum, h).start()
+
+            @pl.when(z < z_size - 1)
+            def _():
+                plane_sum[h] = plane_sum[h] + got
+                z_copy(plane_sum, h).start()
 
     def read(h):
         share = 1.0 / (1.0 + jnp.exp(jnp.full((1, width), -gate[h], F32)))
@@ -259,65 +255,70 @@
     def columns(n):
         return pl.ds(pl.multiple_of(n * tile, tile), tile)
 
-    def project(g):
-        load_w(g).wait()
-        part = pl.ds(pl.multiple_of(g * depth, depth), depth)
+    def project_first():
+        load_w(0).wait()
+        part = pl.ds(0, depth)
 
         def one(n, _):
-            product = dot(attn[:, part], wb[part, columns(n)], (1, 0))
-
-            @pl.when(g == 0)
+            acc[n] = dot(attn[:, part], wb[part, columns(n)], (1, 0))
+            return 0
+
+        lax.fori_loop(0, tiles, one, 0)
+
+    pairs = heads // 2
+
+    def update_pair(j, _):
+        pair = (2 * j, 2 * j + 1)
+        for h in pair:
+            load(k_hbm, kb, k_sem, h).wait()
+            load(v_hbm, vb, v_sem, h).wait()
+        for h in pair:
+            update(h)
+        for h in pair:
+            x_line.begin(own, h)
+        return 0
+
+    lax.fori_loop(0, pairs, update_pair, 0)
+
+    def within(j):
+        return jnp.logical_and(j >= 0, j < pairs)
+
+    def step(i, _):
+        @pl.when(i < pairs)
+        def _():
+            pair = (2 * i, 2 * i + 1)
+            for h in pair:
+                x_line.finish(own, before, row_sum, h, False)
+                y_line.begin(row_sum, h)
+            for h in pair:
+                load(q_hbm, qb, q_sem, h).wait()
+            for h in pair:
+                local(h)
+
+        @pl.when(within(i - 1))
+        def _():
+            for h in (2 * i - 2, 2 * i - 1):
+                y_line.finish(row_sum, before, plane_sum, h, True)
+
+                @pl.when(z == 0)
+                def _():
+                    z_copy(plane_sum, h).start()
+
+        @pl.when(within(i - 1 - z))
+        def _():
+            j = i - 1 - z
+            pair = (2 * j, 2 * j + 1)
+            for h in pair:
+                z_stage(h)
+            for h in pair:
+                read(h)
+
+            @pl.when(j == GROUP // 2 - 1)
             def _():
-                acc[n] = product
-
-            @pl.when(g > 0)
-            def _():
-                acc[n] = acc[n] + product
-            return 0
-
-        lax.fori_loop(0, tiles, one, 0)
-
-    x_lag, y_lag = 1, 2
-    z_lag = y_lag + 2 * z
-
-    def within(h):
-        return jnp.logical_and(h >= 0, h < heads)
-
-    def step(i, _):
-        @pl.when(2 * i < heads)
-        def _():
-            update(2 * i)
-            update(2 * i + 1)
-
-        @pl.when(within(i - x_lag))
-        def _():
-            h = i - x_lag
-            x_line.finish(own, before, row_sum, h, False)
-            y_line.begin(row_sum, h)
-
-        @pl.when(within(i - y_lag))
-        def _():
-            y_line.finish(row_sum, before, plane_sum, i - y_lag, True)
-
-        @pl.when(within(i - z_lag))
-        def _():
-            z_stage(i - z_lag)
-
-        @pl.when(i < heads)
-        def _():
-            local(i)
-
-        @pl.when(within(i - z_lag))
-        def _():
-            h = i - z_lag
-            read(h)
-
-            @pl.when(jnp.logical_and(lax.rem(h, GROUP) == GROUP - 1, h < heads - 1))
-            def _():
-                project(h // GROUP)
-        return 0
-
-    lax.fori_loop(0, heads + y_lag + 2 * (z_size - 1), step, 0)
+                project_first()
+        return 0
+
+    lax.fori_loop(0, pairs + z_size, step, 0)
 
     last = pl.ds((groups - 1) * depth, depth)
     load_w(groups - 1).wait()

time: 81.1 us -> 63.5 us (0.78)
  Pallas kernels: 77.8 us -> 60.2 us
    pallas_call x1, Pallas kernels: 77.8 us -> 60.2 us  [on_device(): pl.pallas_call(functools.partial(kernel, sizes, tile), out_shape=jax.Shap...]
where the time goes in v2:
time: 63.5 us; the launch traced here: 63.3 us
  Pallas kernels  60.2 us (95%)
  local copies, waits for them, and re-layouts  3.13 us (5%)
    pallas_call x1, Pallas kernels, on_device(): pl.pallas_call(functools.partial(kernel, sizes, tile), out_shape=jax.Shap...  60.2 us
    unnamed x1, local copies, waits for them, and re-layouts  3.13 us

profile of v2, /device:TPU:25, one launch (start us, length us, event | category | flops | bytes accessed | tf_op | source)
XLA Modules:
  0.0 63.3 jit_solution(16825073754346397860)
XLA Ops:
  0.0 60.2 %shard_map.55 = bf16[256,4096]{1,0:T(8,128)(2,1)} custom-call(f32[16]{0:T(128)} %gate.1, bf16[512,2048]{1,0:T(8,128)(2,1)} %q_hbm.1, bf16[512,2048]{1,0:T(8,128)(2,1)} %k_hbm.1, bf16[512,2048]{1,0:T(8,128)(2,1)} %v_hbm.1, bf16[2048,4096]{1,0:T(8,128)(2,1)} %w_hbm.1), custom_call_target="tpu_custom_call" | custom-call | flops 10200547328 | bytes 25165824 | tf_op jit(solution)/shard_map/pallas_call | solution.py:394
  60.2 3.1 %copy.7 = bf16[256,4096]{1,0:T(8,128)(2,1)} copy(bf16[256,4096]{1,0:T(8,128)(2,1)} %shard_map.55) | data formatting | bytes 4194304

commit v3 on v2

--- a/solution.py
+++ b/solution.py
@@ -115,6 +115,8 @@
 
 
 GROUP = 8
+PAD = 16
+LEAD = 2
 
 
 def kernel(sizes, tile, gate, q_hbm, k_hbm, v_hbm, w_hbm, o_hbm, *scratch):
@@ -126,7 +128,7 @@
         del scratch[:count]
         return taken
 
-    qb, kb, vb, wb, loc, attn, acc, peer, outb = take(9)
+    qb, kb, vb, vt, wb, loc, attn, acc, peer, outb = take(10)
     own, row_sum, plane_sum, before, z_in = take(5)
     q_sem, k_sem, v_sem, w_sem, o_sem = take(5)
     z_send, z_recv, peer_send, peer_recv = take(4)
@@ -201,33 +203,29 @@
 
     def update(h):
         lift_key = lifted(kb[h].astype(F32)).astype(BF16)
-        own[h, pl.ds(0, width), :] = dot(lift_key, vb[h], (0, 0))
-        zsum = jnp.sum(lift_key.astype(F32), axis=0, keepdims=True)
-        own[h, pl.ds(width, 8), :] = jnp.broadcast_to(zsum, (8, width))
+        vt[h, pl.ds(0, width), :] = vb[h].T
+        vt[h, pl.ds(width, PAD), :] = jnp.ones((PAD, rows), BF16)
+        own[h] = dot(vt[h], lift_key, (1, 0))[:width + 8]
 
     def local(h):
         rate = 1.4426950408889634 / (width ** 0.5)
-        keep = 1.0 / (1.0 + jnp.exp(jnp.full((1, width), gate[h], F32)))
+        keep = 1.0 / (1.0 + jnp.exp(jnp.full((1, half), gate[h], F32)))
         causal = (lax.broadcasted_iota(jnp.int32, (half, half), 0)
-                  >= lax.broadcasted_iota(jnp.int32, (half, half), 1))
+                  <= lax.broadcasted_iota(jnp.int32, (half, half), 1))
         for part in range(2):
-            rows_here = pl.ds(part * half, half)
-            qs = qb[h, rows_here, :]
-            diag = jnp.where(causal, dot(qs, kb[h, rows_here, :], (1, 1)), -jnp.inf)
-            top = jnp.max(diag, axis=-1, keepdims=True)
+            here = pl.ds(part * half, half)
+            qs = qb[h, here, :]
+            diag = jnp.where(causal, dot(kb[h, here, :], qs, (1, 1)), -jnp.inf)
+            top = jnp.max(diag, axis=0, keepdims=True)
             if part == 1:
-                past = dot(qs, kb[h, pl.ds(0, half), :], (1, 1))
-                top = jnp.maximum(top, jnp.max(past, axis=-1, keepdims=True))
-                past = jnp.exp2((past - top) * rate)
-            diag = jnp.exp2((diag - top) * rate)
-            total = jnp.sum(diag, axis=-1, keepdims=True)
+                past = dot(kb[h, pl.ds(0, half), :], qs, (1, 1))
+                top = jnp.maximum(top, jnp.max(past, axis=0, keepdims=True))
+                past = jnp.exp2((past - top) * rate).astype(BF16)
+            diag = jnp.exp2((diag - top) * rate).astype(BF16)
+            out = dot(vt[h, :, here], diag, (1, 0))
             if part == 1:
-                total = total + jnp.sum(past, axis=-1, keepdims=True)
-            inverse = 1.0 / total
-            out = dot((diag * inverse).astype(BF16), vb[h, rows_here, :], (1, 0))
-            if part == 1:
-                out = out + dot((past * inverse).astype(BF16), vb[h, pl.ds(0, half), :], (1, 0))
-            loc[h, rows_here, :] = out * keep
+                out = out + dot(vt[h, :, pl.ds(0, half)], past, (1, 0))
+            loc[h, :, here] = out[:width] * (keep / out[width:width + 1])
 
     def z_stage(h):
         @pl.when(z > 0)
@@ -242,15 +240,19 @@
                 z_copy(plane_sum, h).start()
 
     def read(h):
-        share = 1.0 / (1.0 + jnp.exp(jnp.full((1, width), -gate[h], F32)))
+        share = 1.0 / (1.0 + jnp.exp(jnp.full((1, rows), -gate[h], F32)))
         lift_query = lifted(qb[h].astype(F32)).astype(BF16)
+        norm = before[h, pl.ds(width, 1), :]
+        high = norm.astype(BF16).astype(F32)
+        middle = (norm - high).astype(BF16).astype(F32)
+        low = norm - high - middle
+        row = lax.broadcasted_iota(jnp.int32, (PAD, width), 0)
+        parts = jnp.where(row == 0, high, jnp.where(row == 1, middle, jnp.where(row == 2, low, 0.0)))
         memory = before[h, pl.ds(0, width), :].astype(BF16)
-        numerator = dot(lift_query, memory, (1, 0))
-        norm = before[h, pl.ds(width, 1), :]
-        denominator = jnp.sum(lift_query.astype(F32) * norm, axis=-1, keepdims=True)
-        inverse = 1.0 / jnp.maximum(denominator, 1.0)
-        value = numerator * inverse * share + loc[h]
-        attn[:, pl.ds(pl.multiple_of(h * width, width), width)] = value.astype(BF16)
+        got = dot(jnp.concatenate([memory, parts.astype(BF16)], axis=0), lift_query, (1, 1))
+        denominator = jnp.sum(got[width:width + 8], axis=0, keepdims=True)
+        value = got[:width] * (share / jnp.maximum(denominator, 1.0)) + loc[h]
+        attn[:, pl.ds(pl.multiple_of(h * width, width), width)] = value.astype(BF16).T
 
     def columns(n):
         return pl.ds(pl.multiple_of(n * tile, tile), tile)
@@ -267,18 +269,26 @@
 
     pairs = heads // 2
 
-    def update_pair(j, _):
-        pair = (2 * j, 2 * j + 1)
-        for h in pair:
+    def arrived(j):
+        for h in (2 * j, 2 * j + 1):
             load(k_hbm, kb, k_sem, h).wait()
             load(v_hbm, vb, v_sem, h).wait()
-        for h in pair:
+
+    def update_pair(j):
+        for h in (2 * j, 2 * j + 1):
             update(h)
-        for h in pair:
+
+    def begin_pair(j):
+        for h in (2 * j, 2 * j + 1):
             x_line.begin(own, h)
-        return 0
-
-    lax.fori_loop(0, pairs, update_pair, 0)
+
+    def lead(j, _):
+        arrived(j)
+        update_pair(j)
+        begin_pair(j)
+        return 0
+
+    lax.fori_loop(0, LEAD, lead, 0)
 
     def within(j):
         return jnp.logical_and(j >= 0, j < pairs)
@@ -286,13 +296,21 @@
     def step(i, _):
         @pl.when(i < pairs)
         def _():
-            pair = (2 * i, 2 * i + 1)
-            for h in pair:
+            for h in (2 * i, 2 * i + 1):
                 x_line.finish(own, before, row_sum, h, False)
                 y_line.begin(row_sum, h)
-            for h in pair:
+            for h in (2 * i, 2 * i + 1):
                 load(q_hbm, qb, q_sem, h).wait()
-            for h in pair:
+
+        @pl.when(i < pairs - LEAD)
+        def _():
+            arrived(i + LEAD)
+            update_pair(i + LEAD)
+            begin_pair(i + LEAD)
+
+        @pl.when(i < pairs)
+        def _():
+            for h in (2 * i, 2 * i + 1):
                 local(h)
 
         @pl.when(within(i - 1))
@@ -380,8 +398,9 @@
     blocks = pltpu.VMEM((heads, rows, width), BF16)
     scratch = [
         blocks, blocks, blocks,
+        pltpu.VMEM((heads, width + PAD, rows), BF16),
         pltpu.VMEM(out_weight.shape, BF16),
-        pltpu.VMEM((heads, rows, width), F32),
+        pltpu.VMEM((heads, width, rows), F32),
         pltpu.VMEM((rows, feat), BF16),
         pltpu.VMEM((tiles, rows, tile), F32),
         pltpu.VMEM((tiles, rows // 2, tile), F32),

time: 63.5 us -> 63.1 us (level)
  no operation moved by 1% of the time
where the time goes in v3:
time: 63.1 us; the launch traced here: 63 us
  Pallas kernels  59.9 us (95%)
  local copies, waits for them, and re-layouts  3.13 us (5%)
    pallas_call x1, Pallas kernels, on_device(): pl.pallas_call(functools.partial(kernel, sizes, tile), out_shape=jax.Shap...  59.9 us
    unnamed x1, local copies, waits for them, and re-layouts  3.13 us

profile of v3, /device:TPU:25, one launch (start us, length us, event | category | flops | bytes accessed | tf_op | source)
XLA Modules:
  0.0 63.0 jit_solution(12191927646510401886)
XLA Ops:
  0.0 59.9 %shard_map.55 = bf16[256,4096]{1,0:T(8,128)(2,1)} custom-call(f32[16]{0:T(128)} %gate.1, bf16[512,2048]{1,0:T(8,128)(2,1)} %q_hbm.1, bf16[512,2048]{1,0:T(8,128)(2,1)} %k_hbm.1, bf16[512,2048]{1,0:T(8,128)(2,1)} %v_hbm.1, bf16[2048,4096]{1,0:T(8,128)(2,1)} %w_hbm.1), custom_call_target="tpu_custom_call" | custom-call | flops 10200547328 | bytes 25165824 | tf_op jit(solution)/shard_map/pallas_call | solution.py:413
  59.9 3.1 %copy.7 = bf16[256,4096]{1,0:T(8,128)(2,1)} copy(bf16[256,4096]{1,0:T(8,128)(2,1)} %shard_map.55) | data formatting | bytes 4194304

commit v4 on v3

--- a/solution.py
+++ b/solution.py
@@ -116,7 +116,7 @@
 
 GROUP = 8
 PAD = 16
-LEAD = 2
+LEAD = 4
 
 
 def kernel(sizes, tile, gate, q_hbm, k_hbm, v_hbm, w_hbm, o_hbm, *scratch):
@@ -173,9 +173,7 @@
         load_w(g).start()
         return 0
 
-    lax.fori_loop(0, heads, start_loads, 0)
-    lax.fori_loop(0, heads, start_queries, 0)
-    lax.fori_loop(0, groups, start_weights, 0)
+    lax.fori_loop(0, LEAD, start_loads, 0)
 
     barrier = pltpu.get_barrier_semaphore()
     pl.semaphore_signal(barrier, inc=1, device_id=(seq, other), device_id_type=MESH)
@@ -220,12 +218,16 @@
             if part == 1:
                 past = dot(kb[h, pl.ds(0, half), :], qs, (1, 1))
                 top = jnp.maximum(top, jnp.max(past, axis=0, keepdims=True))
-                past = jnp.exp2((past - top) * rate).astype(BF16)
-            diag = jnp.exp2((diag - top) * rate).astype(BF16)
-            out = dot(vt[h, :, here], diag, (1, 0))
+                past = jnp.exp2((past - top) * rate)
+            diag = jnp.exp2((diag - top) * rate)
+            total = jnp.sum(diag, axis=0, keepdims=True)
             if part == 1:
-                out = out + dot(vt[h, :, pl.ds(0, half)], past, (1, 0))
-            loc[h, :, here] = out[:width] * (keep / out[width:width + 1])
+                total = total + jnp.sum(past, axis=0, keepdims=True)
+            inverse = 1.0 / total
+            out = dot(vt[h, pl.ds(0, width), here], (diag * inverse).astype(BF16), (1, 0))
+            if part == 1:
+                out = out + dot(vt[h, pl.ds(0, width), pl.ds(0, half)], (past * inverse).astype(BF16), (1, 0))
+            loc[h, :, here] = out * keep
 
     def z_stage(h):
         @pl.when(z > 0)
@@ -267,76 +269,72 @@
 
         lax.fori_loop(0, tiles, one, 0)
 
-    pairs = heads // 2
-
-    def arrived(j):
-        for h in (2 * j, 2 * j + 1):
+    def update_pair(first):
+        for h in (first, first + 1):
             load(k_hbm, kb, k_sem, h).wait()
             load(v_hbm, vb, v_sem, h).wait()
-
-    def update_pair(j):
-        for h in (2 * j, 2 * j + 1):
+        for h in (first, first + 1):
             update(h)
 
-    def begin_pair(j):
-        for h in (2 * j, 2 * j + 1):
-            x_line.begin(own, h)
-
-    def lead(j, _):
-        arrived(j)
-        update_pair(j)
-        begin_pair(j)
-        return 0
-
-    lax.fori_loop(0, LEAD, lead, 0)
-
-    def within(j):
-        return jnp.logical_and(j >= 0, j < pairs)
-
-    def step(i, _):
-        @pl.when(i < pairs)
-        def _():
-            for h in (2 * i, 2 * i + 1):
-                x_line.finish(own, before, row_sum, h, False)
-                y_line.begin(row_sum, h)
-            for h in (2 * i, 2 * i + 1):
-                load(q_hbm, qb, q_sem, h).wait()
-
-        @pl.when(i < pairs - LEAD)
-        def _():
-            arrived(i + LEAD)
-            update_pair(i + LEAD)
-            begin_pair(i + LEAD)
-
-        @pl.when(i < pairs)
-        def _():
-            for h in (2 * i, 2 * i + 1):
-                local(h)
-
-        @pl.when(within(i - 1))
-        def _():
-            for h in (2 * i - 2, 2 * i - 1):
-                y_line.finish(row_sum, before, plane_sum, h, True)
-
-                @pl.when(z == 0)
-                def _():
-                    z_copy(plane_sum, h).start()
-
-        @pl.when(within(i - 1 - z))
-        def _():
-            j = i - 1 - z
-            pair = (2 * j, 2 * j + 1)
-            for h in pair:
-                z_stage(h)
-            for h in pair:
-                read(h)
-
-            @pl.when(j == GROUP // 2 - 1)
+    update_pair(0)
+    x_line.begin(own, 0)
+    x_line.begin(own, 1)
+    lax.fori_loop(LEAD, heads, start_loads, 0)
+    lax.fori_loop(0, heads, start_queries, 0)
+    lax.fori_loop(0, groups, start_weights, 0)
+    update_pair(2)
+
+    def within(h):
+        return jnp.logical_and(h >= 0, h < heads)
+
+    def step(t, _):
+        even = lax.rem(t, 2) == 0
+
+        @pl.when(t < heads)
+        def _():
+            x_line.finish(own, before, row_sum, t, False)
+            y_line.begin(row_sum, t)
+
+        @pl.when(t < heads - 2)
+        def _():
+            x_line.begin(own, t + 2)
+
+        @pl.when(within(t - 2))
+        def _():
+            y_line.finish(row_sum, before, plane_sum, t - 2, True)
+
+            @pl.when(z == 0)
+            def _():
+                z_copy(plane_sum, t - 2).start()
+
+        h = t - 2 - z
+
+        @pl.when(within(h))
+        def _():
+            z_stage(h)
+
+        @pl.when(jnp.logical_and(even, t < heads))
+        def _():
+            for head in (t, t + 1):
+                load(q_hbm, qb, q_sem, head).wait()
+            for head in (t, t + 1):
+                local(head)
+
+        @pl.when(jnp.logical_and(jnp.logical_not(even), t < heads - LEAD))
+        def _():
+            update_pair(t + 3)
+
+        @pl.when(jnp.logical_and(within(h), lax.rem(h, 2) == 1))
+        def _():
+            read(h - 1)
+            read(h)
+
+            @pl.when(h == GROUP - 1)
             def _():
                 project_first()
         return 0
 
-    lax.fori_loop(0, pairs + z_size, step, 0)
+    lax.fori_loop(0, heads + 1 + z_size, step, 0)
 
     last = pl.ds((groups - 1) * depth, depth)
     load_w(groups - 1).wait()

time: 63.1 us -> 64.1 us (1.016)
  Pallas kernels: 59.9 us -> 60.9 us
    pallas_call x1, Pallas kernels: 59.9 us -> 60.9 us  [on_device(): pl.pallas_call(functools.partial(kernel, sizes, tile), out_shape=jax.Shap...]
where the time goes in v4:
time: 64.1 us; the launch traced here: 64 us
  Pallas kernels  60.9 us (95%)
  local copies, waits for them, and re-layouts  3.13 us (5%)
    pallas_call x1, Pallas kernels, on_device(): pl.pallas_call(functools.partial(kernel, sizes, tile), out_shape=jax.Shap...  60.9 us
    unnamed x1, local copies, waits for them, and re-layouts  3.13 us

profile of v4, /device:TPU:25, one launch (start us, length us, event | category | flops | bytes accessed | tf_op | source)
XLA Modules:
  0.0 64.0 jit_solution(8775466111130381394)
XLA Ops:
  0.0 60.9 %shard_map.55 = bf16[256,4096]{1,0:T(8,128)(2,1)} custom-call(f32[16]{0:T(128)} %gate.1, bf16[512,2048]{1,0:T(8,128)(2,1)} %q_hbm.1, bf16[512,2048]{1,0:T(8,128)(2,1)} %k_hbm.1, bf16[512,2048]{1,0:T(8,128)(2,1)} %v_hbm.1, bf16[2048,4096]{1,0:T(8,128)(2,1)} %w_hbm.1), custom_call_target="tpu_custom_call" | custom-call | flops 10200547328 | bytes 25165824 | tf_op jit(solution)/shard_map/pallas_call | solution.py:411
  60.9 3.1 %copy.7 = bf16[256,4096]{1,0:T(8,128)(2,1)} copy(bf16[256,4096]{1,0:T(8,128)(2,1)} %shard_map.55) | data formatting | bytes 4194304

commit v5 on v4

--- a/solution.py
+++ b/solution.py
@@ -116,7 +116,7 @@
 
 GROUP = 8
 PAD = 16
-LEAD = 4
+LEAD = 6
 
 
 def kernel(sizes, tile, gate, q_hbm, k_hbm, v_hbm, w_hbm, o_hbm, *scratch):
@@ -194,9 +194,13 @@
         greeted = greeted + (place > 0).astype(jnp.int32) + (place < size - 1).astype(jnp.int32)
     pl.semaphore_wait(barrier, greeted)
 
-    def z_copy(src, h):
+    cut = width // 2
+    pieces = ((0, pl.ds(0, cut)), (1, pl.ds(cut, width + 8 - cut)))
+
+    def z_copy(src, h, piece):
+        index, part = piece
         return pltpu.make_async_remote_copy(
-            src.at[h], z_in.at[h], z_send.at[h], z_recv.at[h],
+            src.at[h, part, :], z_in.at[h, part, :], z_send.at[index, h], z_recv.at[index, h],
             device_id=at(x, y, jnp.minimum(z + 1, z_size - 1)), device_id_type=MESH)
 
     def update(h):
@@ -232,14 +236,16 @@
     def z_stage(h):
         @pl.when(z > 0)
         def _():
-            z_copy(plane_sum, h).wait_recv()
-            got = z_in[h]
-            before[h] = before[h] + got
-
-            @pl.when(z < z_size - 1)
-            def _():
-                plane_sum[h] = plane_sum[h] + got
-                z_copy(plane_sum, h).start()
+            for piece in pieces:
+                part = piece[1]
+                z_copy(plane_sum, h, piece).wait_recv()
+                got = z_in[h, part, :]
+                before[h, part, :] = before[h, part, :] + got
+
+                @pl.when(z < z_size - 1)
+                def _():
+                    plane_sum[h, part, :] = plane_sum[h, part, :] + got
+                    z_copy(plane_sum, h, piece).start()
 
     def read(h):
         share = 1.0 / (1.0 + jnp.exp(jnp.full((1, rows), -gate[h], F32)))
@@ -283,6 +289,9 @@
     lax.fori_loop(0, heads, start_queries, 0)
     lax.fori_loop(0, groups, start_weights, 0)
     update_pair(2)
+    x_line.begin(own, 2)
+    x_line.begin(own, 3)
+    update_pair(4)
 
     def within(h):
         return jnp.logical_and(h >= 0, h < heads)
@@ -295,9 +304,9 @@
             x_line.finish(own, before, row_sum, t, False)
             y_line.begin(row_sum, t)
 
-        @pl.when(t < heads - 2)
-        def _():
-            x_line.begin(own, t + 2)
+        @pl.when(t < heads - 4)
+        def _():
+            x_line.begin(own, t + 4)
 
         @pl.when(within(t - 2))
         def _():
@@ -305,7 +314,8 @@
 
             @pl.when(z == 0)
             def _():
-                z_copy(plane_sum, t - 2).start()
+                for piece in pieces:
+                    z_copy(plane_sum, t - 2, piece).start()
 
         h = t - 2 - z
 
@@ -322,7 +332,7 @@
 
         @pl.when(jnp.logical_and(jnp.logical_not(even), t < heads - LEAD))
         def _():
-            update_pair(t + 3)
+            update_pair(t + 5)
 
         @pl.when(jnp.logical_and(within(h), lax.rem(h, 2) == 1))
         def _():
@@ -370,7 +380,8 @@
 
         @pl.when(z < z_size - 1)
         def _():
-            z_copy(plane_sum, h).wait_send()
+            for piece in pieces:
+                z_copy(plane_sum, h, piece).wait_send()
         return 0
 
     def drain_tiles(n, _):
@@ -405,7 +416,7 @@
         pltpu.VMEM((rows // 2, model), BF16),
         box, box, box, box, box,
         sem, sem, sem, pltpu.SemaphoreType.DMA((heads // GROUP,)), tile_sem,
-        sem, sem, tile_sem, tile_sem,
+        pltpu.SemaphoreType.DMA((2, heads)), pltpu.SemaphoreType.DMA((2, heads)), tile_sem, tile_sem,
     ] + line_scratch(sizes[0], heads, state) + line_scratch(sizes[1], heads, state)
     hbm = pl.BlockSpec(memory_space=pl.ANY)
     return pl.pallas_call(

time: 64.1 us -> 63.3 us (0.988)
  Pallas kernels: 60.9 us -> 60 us
    pallas_call x1, Pallas kernels: 60.9 us -> 60 us  [on_device(): pl.pallas_call(functools.partial(kernel, sizes, tile), out_shape=jax.Shap...]
where the time goes in v5:
time: 63.3 us; the launch traced here: 63.1 us
  Pallas kernels  60 us (95%)
  local copies, waits for them, and re-layouts  3.13 us (5%)
    pallas_call x1, Pallas kernels, on_device(): pl.pallas_call(functools.partial(kernel, sizes, tile), out_shape=jax.Shap...  60 us
    unnamed x1, local copies, waits for them, and re-layouts  3.13 us

profile of v5, /device:TPU:25, one launch (start us, length us, event | category | flops | bytes accessed | tf_op | source)
XLA Modules:
  0.0 63.1 jit_solution(11480429146728990013)
XLA Ops:
  0.0 60.0 %shard_map.55 = bf16[256,4096]{1,0:T(8,128)(2,1)} custom-call(f32[16]{0:T(128)} %gate.1, bf16[512,2048]{1,0:T(8,128)(2,1)} %q_hbm.1, bf16[512,2048]{1,0:T(8,128)(2,1)} %k_hbm.1, bf16[512,2048]{1,0:T(8,128)(2,1)} %v_hbm.1, bf16[2048,4096]{1,0:T(8,128)(2,1)} %w_hbm.1), custom_call_target="tpu_custom_call" | custom-call | flops 10200547328 | bytes 25165824 | tf_op jit(solution)/shard_map/pallas_call | solution.py:422
  60.0 3.1 %copy.7 = bf16[256,4096]{1,0:T(8,128)(2,1)} copy(bf16[256,4096]{1,0:T(8,128)(2,1)} %shard_map.55) | data formatting | bytes 4194304

commit v6 on v5

--- a/solution.py
+++ b/solution.py
@@ -296,6 +296,9 @@
     def within(h):
         return jnp.logical_and(h >= 0, h < heads)
 
+    late = max(heads - 4, z_size + 1)
+    read_lag = jnp.where(z == z_size - 1, z_size + 1, late)
+
     def step(t, _):
         even = lax.rem(t, 2) == 0
 
@@ -334,17 +337,19 @@
         def _():
             update_pair(t + 5)
 
-        @pl.when(jnp.logical_and(within(h), lax.rem(h, 2) == 1))
-        def _():
-            read(h - 1)
-            read(h)
-
-            @pl.when(h == GROUP - 1)
+        ready = t - read_lag
+
+        @pl.when(jnp.logical_and(within(ready), lax.rem(ready, 2) == 1))
+        def _():
+            read(ready - 1)
+            read(ready)
+
+            @pl.when(ready == GROUP - 1)
             def _():
                 project_first()
         return 0
 
-    lax.fori_loop(0, heads + 1 + z_size, step, 0)
+    lax.fori_loop(0, heads + late, step, 0)
 
     last = pl.ds((groups - 1) * depth, depth)
     load_w(groups - 1).wait()

time: 63.3 us -> 62.8 us (level)
  the two profiles are of different devices: /device:TPU:25 before, /device:TPU:17 now
where the time goes in v6:
time: 62.8 us; the launch traced here: 62.7 us
  Pallas kernels  59.5 us (95%)
  local copies, waits for them, and re-layouts  3.13 us (5%)
    pallas_call x1, Pallas kernels, on_device(): pl.pallas_call(functools.partial(kernel, sizes, tile), out_shape=jax.Shap...  59.5 us
    unnamed x1, local copies, waits for them, and re-layouts  3.13 us

profile of v6, /device:TPU:17, one launch (start us, length us, event | category | flops | bytes accessed | tf_op | source)
XLA Modules:
  0.0 62.7 jit_solution(7510356880314086973)
XLA Ops:
  0.0 59.5 %shard_map.55 = bf16[256,4096]{1,0:T(8,128)(2,1)} custom-call(f32[16]{0:T(128)} %gate.1, bf16[512,2048]{1,0:T(8,128)(2,1)} %q_hbm.1, bf16[512,2048]{1,0:T(8,128)(2,1)} %k_hbm.1, bf16[512,2048]{1,0:T(8,128)(2,1)} %v_hbm.1, bf16[2048,4096]{1,0:T(8,128)(2,1)} %w_hbm.1), custom_call_target="tpu_custom_call" | custom-call | flops 10200547328 | bytes 25165824 | tf_op jit(solution)/shard_map/pallas_call | solution.py:427
  59.5 3.1 %copy.7 = bf16[256,4096]{1,0:T(8,128)(2,1)} copy(bf16[256,4096]{1,0:T(8,128)(2,1)} %shard_map.55) | data formatting | bytes 4194304

commit v7 on v6

--- a/solution.py
+++ b/solution.py
@@ -265,15 +265,12 @@
     def columns(n):
         return pl.ds(pl.multiple_of(n * tile, tile), tile)
 
-    def project_first():
-        load_w(0).wait()
+    per_step = tiles // (heads - GROUP)
+    assert per_step * (heads - GROUP) == tiles
+
+    def project_first(n):
         part = pl.ds(0, depth)
-
-        def one(n, _):
-            acc[n] = dot(attn[:, part], wb[part, columns(n)], (1, 0))
-            return 0
-
-        lax.fori_loop(0, tiles, one, 0)
+        acc[n] = dot(attn[:, part], wb[part, columns(n)], (1, 0))
 
     def update_pair(first):
         for h in (first, first + 1):
@@ -297,7 +294,7 @@
         return jnp.logical_and(h >= 0, h < heads)
 
     late = max(heads - 4, z_size + 1)
-    read_lag = jnp.where(z == z_size - 1, z_size + 1, late)
+    read_lag = jnp.where(z == z_size - 1, z_size + 1, late - 2 * z)
 
     def step(t, _):
         even = lax.rem(t, 2) == 0
@@ -346,7 +343,12 @@
 
             @pl.when(ready == GROUP - 1)
             def _():
-                project_first()
+                load_w(0).wait()
+
+        @pl.when(jnp.logical_and(ready >= GROUP, ready < heads))
+        def _():
+            for piece in range(per_step):
+                project_first((ready - GROUP) * per_step + piece)
         return 0
 
     lax.fori_loop(0, heads + late, step, 0)

time: 62.8 us -> 59.9 us (0.954)
  the two profiles are of different devices: /device:TPU:17 before, /device:TPU:25 now
where the time goes in v7:
time: 59.9 us; the launch traced here: 58.8 us
  Pallas kernels  55.6 us (93%)
  local copies, waits for them, and re-layouts  3.13 us (5%)
    pallas_call x1, Pallas kernels, on_device(): pl.pallas_call(functools.partial(kernel, sizes, tile), out_shape=jax.Shap...  55.6 us
    unnamed x1, local copies, waits for them, and re-layouts  3.13 us

profile of v7, /device:TPU:25, one launch (start us, length us, event | category | flops | bytes accessed | tf_op | source)
XLA Modules:
  0.0 58.8 jit_solution(425715143837599125)
XLA Ops:
  0.0 55.6 %shard_map.55 = bf16[256,4096]{1,0:T(8,128)(2,1)} custom-call(f32[16]{0:T(128)} %gate.1, bf16[512,2048]{1,0:T(8,128)(2,1)} %q_hbm.1, bf16[512,2048]{1,0:T(8,128)(2,1)} %k_hbm.1, bf16[512,2048]{1,0:T(8,128)(2,1)} %v_hbm.1, bf16[2048,4096]{1,0:T(8,128)(2,1)} %w_hbm.1), custom_call_target="tpu_custom_call" | custom-call | flops 10200547328 | bytes 25165824 | tf_op jit(solution)/shard_map/pallas_call | solution.py:429
  55.6 3.1 %copy.7 = bf16[256,4096]{1,0:T(8,128)(2,1)} copy(bf16[256,4096]{1,0:T(8,128)(2,1)} %shard_map.55) | data formatting | bytes 4194304
